TPU v7x, 256 devices: a whole 4x4x8 slice. The times are simulated.
256 devices in a mesh: seq: 32 (over y, x, core), head: 8 (over z).
Axes of the slice: x: 4, y: 4, z: 8, core: 2. Of those that a mesh axis runs over, the one named last changes fastest.
Arguments:
- tokens: bfloat16 [8192, 2048], P('seq'), may hold values from -60 to 60
- w_query: bfloat16 [2048, 2048], P(None, 'head'), may hold values from -2 to 2
- w_key: bfloat16 [2048, 2048], P(None, 'head'), may hold values from -2 to 2
- w_value: bfloat16 [2048, 2048], P(None, 'head'), may hold values from -0.125 to 0.125
- w_out: bfloat16 [2048, 2048], P('head'), may hold values from -0.125 to 0.125
Outputs:
- mixed: bfloat16 [8192, 2048], P(('seq', 'head'))
All inputs are finite; a program needn't handle non-finite values.
Results may differ from a plain program's by a relative error of at most 0.019.
The roundings to bfloat16 on the way count: a program that leaves them out, or rounds other values in their place, can miss the bound.
Values may be sent and summed in bfloat16 or wider, within the bound.
A program may use at most 128 MiB of HBM per device.

v0:
```python
import math

import jax
import jax.numpy as jnp
from jax import lax
from jax.sharding import PartitionSpec as P

HEAD_DIM = 128
LEAF = 128


LN_TWO = math.log(2.0)


def swapped(block, axis, stride):
    count = lax.axis_size(axis)
    route = []
    for low in range(count):
        high = low | 1 << stride
        if high != low and high < count:
            route += [(low, high), (high, low)]
    return lax.ppermute(block, axis, route)


def coarsen(array, factor):
    wide = array.astype(jnp.float32)
    return wide.reshape((wide.shape[0] // factor, factor) + wide.shape[1:]).mean(axis=1)


def sibling_blocks(array):
    count = array.shape[0]
    paired = array.reshape((count // 2, 2) + array.shape[1:])
    return jnp.flip(paired, axis=1).reshape(array.shape)


def flatten_stats(top, total, summed, query_rows):
    rows = query_rows.shape[0] * query_rows.shape[1]
    top = jnp.transpose(top, (0, 2, 1)).reshape(rows, query_rows.shape[2])
    total = jnp.transpose(total, (0, 2, 1)).reshape(rows, query_rows.shape[2])
    return (top, total, summed.reshape(rows, query_rows.shape[2], query_rows.shape[3]))


def near_field(query_rows, key_rows, value_rows):
    both_keys = jnp.concatenate([key_rows, sibling_blocks(key_rows)], axis=1)
    both_values = jnp.concatenate([value_rows, sibling_blocks(value_rows)], axis=1)
    scale_factor = 1.0 / math.sqrt(HEAD_DIM)
    score_matrix = (
        jnp.einsum("ogxt,opxt->oxgp", query_rows, both_keys, preferred_element_type=jnp.float32)
        * scale_factor
    )
    top = jnp.max(score_matrix, axis=-1)
    weights = jnp.exp(score_matrix - top[..., None])
    total = jnp.sum(weights, axis=-1)
    rounded = weights.astype(jnp.bfloat16)
    summed = jnp.einsum("bhqk,bkhd->bqhd", rounded, both_values, preferred_element_type=jnp.float32)
    return flatten_stats(top, total, summed, query_rows)


def distant_field(query_rows, key_rows, value_rows, extra_score):
    scale_factor = 1.0 / math.sqrt(HEAD_DIM)
    score_matrix = (
        jnp.einsum("ogxt,opxt->oxgp", query_rows, key_rows, precision=lax.Precision.HIGHEST)
        * scale_factor
        + extra_score
    )
    top = jnp.max(score_matrix, axis=-1)
    weights = jnp.exp(score_matrix - top[..., None])
    total = jnp.sum(weights, axis=-1)
    summed = jnp.einsum("bhqk,bkhd->bqhd", weights, value_rows, precision=lax.Precision.HIGHEST)
    return flatten_stats(top, total, summed, query_rows)


def expand(part, factor):
    return tuple((jnp.repeat(member, factor, axis=0) for member in part))


def merge_level(state, part):
    newest = jnp.maximum(state[0], part[0])
    old_factor = jnp.exp(state[0] - newest)
    new_factor = jnp.exp(part[0] - newest)
    total = state[1] * old_factor + part[1] * new_factor
    summed = state[2] * old_factor[..., None] + part[2] * new_factor[..., None]
    return (newest, total, summed)


def shards(tokens, w_query, w_key, w_value, w_out):
    rows = tokens.shape[0]
    heads_here = w_query.shape[1] // HEAD_DIM

    def project(weight):
        result = jnp.dot(tokens, weight, preferred_element_type=jnp.float32).astype(jnp.bfloat16)
        return result.reshape(rows, heads_here, HEAD_DIM)

    query_rows, key_rows, value_rows = (project(w_query), project(w_key), project(w_value))
    blocks = rows // LEAF
    state = near_field(
        query_rows.reshape(blocks, LEAF, heads_here, HEAD_DIM),
        key_rows.reshape(blocks, LEAF, heads_here, HEAD_DIM),
        value_rows.reshape(blocks, LEAF, heads_here, HEAD_DIM),
    )
    local_levels = blocks.bit_length() - 1
    own_keys = coarsen(key_rows, blocks)
    own_values = coarsen(value_rows, blocks)
    seq_bits = lax.axis_size("seq").bit_length() - 1
    my_index = lax.axis_index("seq")
    for bit_index in range(seq_bits):
        sib_keys, sib_values = swapped((own_keys, own_values), "seq", bit_index)
        level = local_levels + bit_index
        factor = 2**level
        coarse_query = coarsen(query_rows, factor)[None]
        part = distant_field(coarse_query, sib_keys[None], sib_values[None], level * LN_TWO)
        state = merge_level(state, expand(part, factor))
        if bit_index + 1 < seq_bits:
            upper_half = my_index >> bit_index & 1 == 1
            lower_keys = jnp.where(upper_half, sib_keys, own_keys)
            higher_keys = jnp.where(upper_half, own_keys, sib_keys)
            lower_values = jnp.where(upper_half, sib_values, own_values)
            higher_values = jnp.where(upper_half, own_values, sib_values)
            own_keys = coarsen(jnp.concatenate([lower_keys, higher_keys], axis=0), 2)
            own_values = coarsen(jnp.concatenate([lower_values, higher_values], axis=0), 2)
    attention = (
        (state[2] / state[1][..., None]).astype(jnp.bfloat16).reshape(rows, heads_here * HEAD_DIM)
    )
    return lax.psum_scatter(
        jnp.dot(attention, w_out, preferred_element_type=jnp.float32).astype(jnp.bfloat16),
        "head",
        scatter_dimension=0,
        tiled=True,
    )


def solution(mesh):
    placed = (P("seq", None), P(None, "head"), P(None, "head"), P(None, "head"), P("head", None))
    return jax.shard_map(
        shards, mesh=mesh, in_specs=placed, out_specs=P(("seq", "head"), None), check_vma=False
    )
```

profile of v0, /device:TPU:2, one launch (start us, length us, event | category | flops | bytes accessed | tf_op | source)
XLA Modules:
  0.0 108.8 jit_solution(5965554515272732403)
XLA Ops:
  6.5 2.1 %convolution_convert_fusion.1 = bf16[256,256]{1,0:T(8,128)(2,1)S(1)} fusion(bf16[256,2048]{1,0:T(8,128)(2,1)} %param.5, bf16[2048,256]{1,0:T(8,128)(2,1)} %param.7), kind=kOutput, calls=%fused_computation.3 | convolution fusion | flops 268500992 | bytes 2228224 | tf_op jit(solution)/shard_map/dot_general | solution.py:91
  9.0 0.7 copy_multiply_fusion.1
  9.8 1.7 %convolution_convert_fusion.3 = bf16[256,256]{1,0:T(8,128)(2,1)S(1)} fusion(bf16[256,2048]{1,0:T(8,128)(2,1)S(1)} %copy-done.1, bf16[2048,256]{1,0:T(8,128)(2,1)} %param.8), kind=kOutput, calls=%fused_computation.5 | convolution fusion | flops 268500992 | bytes 2228224 | tf_op jit(solution)/shard_map/dot_general | solution.py:91
  11.9 0.7 copy_multiply_fusion
  12.5 0.3 collective-permute-start.1
  12.9 0.7 reshape_reshape_reshape.6
  13.6 0.7 reshape_reshape_reshape.7
  14.3 2.3 %bitcast_reduce_fusion = (f32[32,2,128]{2,1,0:T(2,128)}, bf16[256,256]{1,0:T(8,128)(2,1)S(1)}) fusion(bf16[256,2048]{1,0:T(8,128)(2,1)S(1)} %copy-done.1, bf16[2048,256]{1,0:T(8,128)(2,1)} %param.6), kind=kOutput, calls=%fused_computation.55 | convolution fusion | flops 268623872 | bytes 2260992 | tf_op jit(solution)/shard_map/dot_general | solution.py:91
  17.7 0.7 reverse_bitcast_fusion.1
  18.3 0.8 copy.107
  19.2 0.3 fusion.64
  19.5 0.5 copy-done.4
  21.4 0.3 reduce_sum.203
  21.7 2.4 %collective-permute-start.2 = (f32[128,2,128]{2,0,1:T(8,128)S(1)}, f32[128,2,128]{2,0,1:T(8,128)S(1)}, u32[]{:S(2)}, u32[]{:S(2)}) collective-permute-start(f32[128,2,128]{2,0,1:T(8,128)S(1)} %broadcast_multiply_fusion.7), channel_id=1, source_target_pairs={{0,16},{16,0},{8,24},{24,8},{32,48},{48,32},{40,56},{56,40},{64,80... | collective-permute-start | bytes 393224 | tf_op jit(solution)/shard_map/ppermute | solution.py:22
  24.1 0.9 broadcast_select_fusion.13
  25.1 0.3 reduce_sum.204
  25.5 0.4 fusion.66
  25.9 1.3 %convolution_bitcast_fusion.1 = f32[128,2,128]{0,2,1:T(8,128)S(1)} fusion(f32[128,2,128]{2,0,1:T(8,128)} %collective-permute-done.1, f32[2,128,128]{1,2,0:T(8,128)S(1)} %get-tuple-element.47, f32[2,128]{1,0:T(2,128)S(1)} %get-tuple-element.46), kind=kOutput, calls=%fused_computation.6 | convolution fusion | flops 50364416 | bytes 394240 | tf_op jit(solution)/shard_map/bhqk,bkhd->bqhd/dot_general | solution.py:69
  28.3 2.4 %collective-permute-start.4 = (f32[128,2,128]{2,0,1:T(8,128)S(1)}, f32[128,2,128]{2,0,1:T(8,128)S(1)}, u32[]{:S(2)}, u32[]{:S(2)}) collective-permute-start(f32[128,2,128]{2,0,1:T(8,128)S(1)} %broadcast_multiply_fusion.5), channel_id=1, source_target_pairs={{0,32},{32,0},{8,40},{40,8},{16,48},{48,16},{24,56},{56,24},{64,96... | collective-permute-start | bytes 393224 | tf_op jit(solution)/shard_map/ppermute | solution.py:22
  30.8 0.3 reduce_sum.207
  31.2 1.6 %collective-permute-start.5 = (f32[128,2,128]{2,0,1:T(8,128)S(1)}, f32[128,2,128]{2,0,1:T(8,128)S(1)}, u32[]{:S(2)}, u32[]{:S(2)}) collective-permute-start(f32[128,2,128]{2,0,1:T(8,128)S(1)} %broadcast_multiply_fusion.4), channel_id=1, source_target_pairs={{0,32},{32,0},{8,40},{40,8},{16,48},{48,16},{24,56},{56,24},{64,96... | collective-permute-start | bytes 393224 | tf_op jit(solution)/shard_map/ppermute | solution.py:22
  32.8 0.4 fusion.65
  34.2 1.8 %collective-permute-done.4 = f32[128,2,128]{2,0,1:T(8,128)S(1)} collective-permute-done((f32[128,2,128]{2,0,1:T(8,128)S(1)}, f32[128,2,128]{2,0,1:T(8,128)S(1)}, u32[]{:S(2)}, u32[]{:S(2)}) %collective-permute-start.4) | collective-permute-done | bytes 131104 | tf_op jit(solution)/shard_map/ppermute | solution.py:22
  36.3 2.0 %collective-permute-start.6 = (f32[128,2,128]{2,0,1:T(8,128)S(1)}, f32[128,2,128]{2,0,1:T(8,128)S(1)}, u32[]{:S(2)}, u32[]{:S(2)}) collective-permute-start(f32[128,2,128]{2,0,1:T(8,128)S(1)} %broadcast_multiply_fusion.3), channel_id=1, source_target_pairs={{0,64},{64,0},{8,72},{72,8},{16,80},{80,16},{24,88},{88,24},{32,96... | collective-permute-start | bytes 393224 | tf_op jit(solution)/shard_map/ppermute | solution.py:22
  38.4 0.3 reduce_sum.210
  38.8 1.2 %collective-permute-start.7 = (f32[128,2,128]{2,0,1:T(8,128)S(1)}, f32[128,2,128]{2,0,1:T(8,128)S(1)}, u32[]{:S(2)}, u32[]{:S(2)}) collective-permute-start(f32[128,2,128]{2,0,1:T(8,128)S(1)} %broadcast_multiply_fusion.2), channel_id=1, source_target_pairs={{0,64},{64,0},{8,72},{72,8},{16,80},{80,16},{24,88},{88,24},{32,96... | collective-permute-start | bytes 393224 | tf_op jit(solution)/shard_map/ppermute | solution.py:22
  40.0 0.4 fusion.63
  41.2 1.5 %collective-permute-done.6 = f32[128,2,128]{2,0,1:T(8,128)S(1)} collective-permute-done((f32[128,2,128]{2,0,1:T(8,128)S(1)}, f32[128,2,128]{2,0,1:T(8,128)S(1)}, u32[]{:S(2)}, u32[]{:S(2)}) %collective-permute-start.6) | collective-permute-done | bytes 131104 | tf_op jit(solution)/shard_map/ppermute | solution.py:22
  43.1 3.5 %collective-permute-start.8 = (f32[128,2,128]{2,0,1:T(8,128)S(1)}, f32[128,2,128]{2,0,1:T(8,128)S(1)}, u32[]{:S(2)}, u32[]{:S(2)}) collective-permute-start(f32[128,2,128]{2,0,1:T(8,128)S(1)} %broadcast_multiply_fusion.1), channel_id=1, source_target_pairs={{0,128},{128,0},{8,136},{136,8},{16,144},{144,16},{24,152},{152,24... | collective-permute-start | bytes 393224 | tf_op jit(solution)/shard_map/ppermute | solution.py:22
  46.6 0.3 reduce_sum.213
  47.0 2.2 %collective-permute-start.9 = (f32[128,2,128]{2,0,1:T(8,128)S(1)}, f32[128,2,128]{2,0,1:T(8,128)S(1)}, u32[]{:S(2)}, u32[]{:S(2)}) collective-permute-start(f32[128,2,128]{2,0,1:T(8,128)S(1)} %broadcast_multiply_fusion), channel_id=1, source_target_pairs={{0,128},{128,0},{8,136},{136,8},{16,144},{144,16},{24,152},{152,24... | collective-permute-start | bytes 393224 | tf_op jit(solution)/shard_map/ppermute | solution.py:22
  49.1 0.4 fusion.62
  50.3 0.4 collective-permute-done.8
  50.7 0.4 fusion.61
  51.3 2.3 %collective-permute-done.9 = f32[128,2,128]{2,0,1:T(8,128)S(1)} collective-permute-done((f32[128,2,128]{2,0,1:T(8,128)S(1)}, f32[128,2,128]{2,0,1:T(8,128)S(1)}, u32[]{:S(2)}, u32[]{:S(2)}) %collective-permute-start.9) | collective-permute-done | bytes 131104 | tf_op jit(solution)/shard_map/ppermute | solution.py:22
  56.0 0.3 div.87
  56.3 0.3 mul.228
  56.6 0.3 mul.236
  57.0 0.3 mul.225
  57.3 0.3 mul.233
  57.7 0.3 mul.241
  58.0 0.3 mul.244
  58.3 0.3 mul.249
  58.7 0.3 mul.252
  59.0 0.3 mul.257
  59.3 0.3 mul.260
  59.8 1.6 %convolution_convert_fusion = bf16[256,2048]{1,0:T(8,128)(2,1)} fusion(bf16[256,2048]{1,0:T(8,128)(2,1)S(1)} %copy-done, f32[32,8,2,128]{3,2,1,0:T(2,128)S(1)} %bitcast.278, f32[32,8,2,128]{3,2,1,0:T(2,128)S(1)} %bitcast.288, f32[32,8,2,128]{3,2,1,0:T(2,128)S(1)} %bitcast.276, f32[32,8,2,128]{3,2,1,0:T(2,128)S(1)} %bitcast.287, ...), kind=kOutput, calls=%fused_computation | convolution fusion | flops 270073856 | bytes 6324224 | tf_op jit(solution)/shard_map/dot_general | solution.py:125
  61.4 40.6 %reduce-scatter.2.cloned.1.call-done = bf16[32,2048]{1,0:T(8,128)(2,1)} async-done(((bf16[256,2048]{1,0:T(8,128)(2,1)}), bf16[32,2048]{1,0:T(8,128)(2,1)}) %reduce-scatter.2.cloned.1.call-update) | async-done | bytes 131088 | tf_op jit(solution)/shard_map/reduce_scatter | solution.py:124
  (122 shorter events, 10.6 us)
Async XLA Ops:
  6.5 53.2 %copy-start = (bf16[256,2048]{1,0:T(8,128)(2,1)S(1)}, bf16[256,2048]{1,0:T(8,128)(2,1)}, u32[]{:S(2)}) copy-start(bf16[256,2048]{1,0:T(8,128)(2,1)} %param.9) | copy-start | bytes 3145732
  6.5 95.5 %reduce-scatter.2.cloned.1.call-start = ((), (), s32[]{:S(2)}) async-start(), calls=%async_computation.1 | async-start | bytes 1179648 | tf_op jit(solution)/shard_map/reduce_scatter | solution.py:124
  8.6 1.2 %copy-start.1 = (bf16[256,2048]{1,0:T(8,128)(2,1)S(1)}, bf16[256,2048]{1,0:T(8,128)(2,1)}, u32[]{:S(2)}) copy-start(bf16[256,2048]{1,0:T(8,128)(2,1)} %param.5) | copy-start | bytes 3145732
  9.7 11.7 %collective-permute-start = (f32[128,2,128]{2,0,1:T(8,128)}, f32[128,2,128]{2,0,1:T(8,128)S(1)}, u32[]{:S(2)}, u32[]{:S(2)}) collective-permute-start(f32[128,2,128]{2,0,1:T(8,128)} %copy_multiply_fusion.1), channel_id=1, source_target_pairs={{0,8},{8,0},{16,24},{24,16},{32,40},{40,32},{48,56},{56,48},{64,72... | collective-permute-start | bytes 393224 | tf_op jit(solution)/shard_map/ppermute | solution.py:22
  12.5 11.6 %collective-permute-start.1 = (f32[128,2,128]{2,0,1:T(8,128)}, f32[128,2,128]{2,0,1:T(8,128)}, u32[]{:S(2)}, u32[]{:S(2)}) collective-permute-start(f32[128,2,128]{2,0,1:T(8,128)} %copy_multiply_fusion), channel_id=1, source_target_pairs={{0,8},{8,0},{16,24},{24,16},{32,40},{40,32},{48,56},{56,48},{64,72... | collective-permute-start | bytes 393224 | tf_op jit(solution)/shard_map/ppermute | solution.py:22
  16.6 0.9 copy-start.3
  16.8 2.3 %copy-start.2 = (bf16[1,2,128,2,128]{4,3,2,1,0:T(2,128)(2,1)S(1)}, bf16[1,2,128,2,128]{4,3,2,1,0:T(2,128)(2,1)}, u32[]{:S(2)}) copy-start(bf16[1,2,128,2,128]{4,3,2,1,0:T(2,128)(2,1)} %reshape_reshape_reshape.7) | copy-start | bytes 393220
  19.1 0.9 copy-start.4
  19.1 1.0 copy-start.5
  21.7 6.2 %collective-permute-start.2 = (f32[128,2,128]{2,0,1:T(8,128)S(1)}, f32[128,2,128]{2,0,1:T(8,128)S(1)}, u32[]{:S(2)}, u32[]{:S(2)}) collective-permute-start(f32[128,2,128]{2,0,1:T(8,128)S(1)} %broadcast_multiply_fusion.7), channel_id=1, source_target_pairs={{0,16},{16,0},{8,24},{24,8},{32,48},{48,32},{40,56},{56,40},{64,80... | collective-permute-start | bytes 393224 | tf_op jit(solution)/shard_map/ppermute | solution.py:22
  25.4 5.4 %collective-permute-start.3 = (f32[128,2,128]{2,0,1:T(8,128)S(1)}, f32[128,2,128]{2,0,1:T(8,128)S(1)}, u32[]{:S(2)}, u32[]{:S(2)}) collective-permute-start(f32[128,2,128]{2,0,1:T(8,128)S(1)} %broadcast_multiply_fusion.6), channel_id=1, source_target_pairs={{0,16},{16,0},{8,24},{24,8},{32,48},{48,32},{40,56},{56,40},{64,80... | collective-permute-start | bytes 393224 | tf_op jit(solution)/shard_map/ppermute | solution.py:22
  28.3 7.6 %collective-permute-start.4 = (f32[128,2,128]{2,0,1:T(8,128)S(1)}, f32[128,2,128]{2,0,1:T(8,128)S(1)}, u32[]{:S(2)}, u32[]{:S(2)}) collective-permute-start(f32[128,2,128]{2,0,1:T(8,128)S(1)} %broadcast_multiply_fusion.5), channel_id=1, source_target_pairs={{0,32},{32,0},{8,40},{40,8},{16,48},{48,16},{24,56},{56,24},{64,96... | collective-permute-start | bytes 393224 | tf_op jit(solution)/shard_map/ppermute | solution.py:22
  31.2 7.2 %collective-permute-start.5 = (f32[128,2,128]{2,0,1:T(8,128)S(1)}, f32[128,2,128]{2,0,1:T(8,128)S(1)}, u32[]{:S(2)}, u32[]{:S(2)}) collective-permute-start(f32[128,2,128]{2,0,1:T(8,128)S(1)} %broadcast_multiply_fusion.4), channel_id=1, source_target_pairs={{0,32},{32,0},{8,40},{40,8},{16,48},{48,16},{24,56},{56,24},{64,96... | collective-permute-start | bytes 393224 | tf_op jit(solution)/shard_map/ppermute | solution.py:22
  36.3 3.7 %copy-start.6 = (f32[32,2,128]{2,1,0:T(2,128)S(1)}, f32[32,2,128]{2,1,0:T(2,128)}, u32[]{:S(2)}) copy-start(f32[32,2,128]{2,1,0:T(2,128)} %get-tuple-element.38) | copy-start | bytes 98308
  36.3 6.4 %collective-permute-start.6 = (f32[128,2,128]{2,0,1:T(8,128)S(1)}, f32[128,2,128]{2,0,1:T(8,128)S(1)}, u32[]{:S(2)}, u32[]{:S(2)}) collective-permute-start(f32[128,2,128]{2,0,1:T(8,128)S(1)} %broadcast_multiply_fusion.3), channel_id=1, source_target_pairs={{0,64},{64,0},{8,72},{72,8},{16,80},{80,16},{24,88},{88,24},{32,96... | collective-permute-start | bytes 393224 | tf_op jit(solution)/shard_map/ppermute | solution.py:22
  38.8 7.8 %collective-permute-start.7 = (f32[128,2,128]{2,0,1:T(8,128)S(1)}, f32[128,2,128]{2,0,1:T(8,128)S(1)}, u32[]{:S(2)}, u32[]{:S(2)}) collective-permute-start(f32[128,2,128]{2,0,1:T(8,128)S(1)} %broadcast_multiply_fusion.2), channel_id=1, source_target_pairs={{0,64},{64,0},{8,72},{72,8},{16,80},{80,16},{24,88},{88,24},{32,96... | collective-permute-start | bytes 393224 | tf_op jit(solution)/shard_map/ppermute | solution.py:22
  43.1 7.6 %collective-permute-start.8 = (f32[128,2,128]{2,0,1:T(8,128)S(1)}, f32[128,2,128]{2,0,1:T(8,128)S(1)}, u32[]{:S(2)}, u32[]{:S(2)}) collective-permute-start(f32[128,2,128]{2,0,1:T(8,128)S(1)} %broadcast_multiply_fusion.1), channel_id=1, source_target_pairs={{0,128},{128,0},{8,136},{136,8},{16,144},{144,16},{24,152},{152,24... | collective-permute-start | bytes 393224 | tf_op jit(solution)/shard_map/ppermute | solution.py:22
  47.0 6.6 %collective-permute-start.9 = (f32[128,2,128]{2,0,1:T(8,128)S(1)}, f32[128,2,128]{2,0,1:T(8,128)S(1)}, u32[]{:S(2)}, u32[]{:S(2)}) collective-permute-start(f32[128,2,128]{2,0,1:T(8,128)S(1)} %broadcast_multiply_fusion), channel_id=1, source_target_pairs={{0,128},{128,0},{8,136},{136,8},{16,144},{144,16},{24,152},{152,24... | collective-permute-start | bytes 393224 | tf_op jit(solution)/shard_map/ppermute | solution.py:22
Sparse Core Ops, SparseCore 0:
  61.6 40.3 reduce-scatter.1
where the time goes:
time: 109 us
  waiting for transfers between devices  46.6 us (43%)
  starting transfers between devices  15.7 us (14%)
  between operations  14.1 us (13%)
  matrix products  12.7 us (12%)
  local copies, waits for them, and re-layouts  12.6 us (12%)
  other arithmetic  7.08 us (6%)
    reduce_scatter x1, waiting for transfers between devices, shards(): lax.psum_scatter(jnp.dot(attention, w_out, preferred_element_type=jnp.flo...  40.6 us
    ppermute x10, starting transfers between devices, swapped(): return lax.ppermute(block, axis, route)  15.7 us
    ppermute x10, waiting for transfers between devices, swapped(): return lax.ppermute(block, axis, route)  6.05 us
    dot_general x3, matrix products, project(): jnp.dot(tokens, weight, preferred_element_type=jnp.float32)  6.02 us
    reduce_sum x14, other arithmetic, coarsen(): wide.reshape((wide.shape[0] // factor, factor) + wide.shape[1:])  3.43 us
    mul x10, local copies, waits for them, and re-layouts, merge_level(): summed = state[2] * old_factor[..., None] + part[2] * new_factor[..., None]  3.35 us
    dot_general x5, matrix products, distant_field(): jnp.einsum('bhqk,bkhd->bqhd', weights, value_rows, precision=lax.Precisio...  2.42 us
  transfers between devices with their start and end apart: 11, of which 6 were waited for; matrix products, arithmetic and copies ran while one was open for 19% of the time, Pallas kernels for 0%

commit v1 on v0

v1 whole, which is shorter than its diff:
```python
import functools
import math

import jax
import jax.numpy as jnp
from jax import lax
from jax.experimental import pallas as pl
from jax.experimental.pallas import tpu as pltpu
from jax.sharding import PartitionSpec as P

HEAD_DIM = 128
ROWS = 256
WIDTH = 256
MODEL = 2048
HALF = MODEL // 2
LEVELS = 5
SEQ = 32
RING = 8
PIECE = ROWS // RING
LOG2_E = 1.4426950408889634
SCORE_SCALE = LOG2_E / math.sqrt(HEAD_DIM)
MESH = pl.DeviceIdType.MESH
BF16 = jnp.bfloat16
F32 = jnp.float32


def dot(a, b):
    return jnp.dot(a, b, preferred_element_type=F32)


def dot_nt(a, b):
    return lax.dot_general(a, b, (((1,), (1,)), ((), ())), preferred_element_type=F32)


def averaging_rows(level):
    row = lax.broadcasted_iota(jnp.int32, (ROWS, ROWS), 0)
    col = lax.broadcasted_iota(jnp.int32, (ROWS, ROWS), 1)
    same = (row >> level) == (col >> level)
    return jnp.where(same, 2.0**-level, 0.0).astype(BF16)


def coarse_matrix():
    row = lax.broadcasted_iota(jnp.int32, (ROWS, ROWS), 0)
    col = lax.broadcasted_iota(jnp.int32, (ROWS, ROWS), 1)
    total = jnp.zeros((ROWS, ROWS), F32)
    start = 0
    for level in range(1, LEVELS + 1):
        count = ROWS >> level
        hit = (row >= start) & (row < start + count) & ((col >> level) == row - start)
        total = jnp.where(hit, 2.0**-level, total)
        start += count
    return total.astype(BF16)


def kernel(
    tok_hbm, wq_hbm, wk_hbm, wv_hbm, wo_hbm, out_ref,
    tok, wq, wk, wv, wo,
    send1, send2, send3, send4, send5,
    land1, land2, land3, land4, land5,
    partial, stage, ring,
    load_sem, send_sem, recv_sem, ring_send, ring_recv,
):
    sends = (send1, send2, send3, send4, send5)
    lands = (land1, land2, land3, land4, land5)
    me = lax.axis_index("seq")
    z = lax.axis_index("head")

    loads = [
        pltpu.make_async_copy(src, dst, load_sem.at[i])
        for i, (src, dst) in enumerate(
            ((tok_hbm, tok), (wk_hbm, wk), (wv_hbm, wv), (wq_hbm, wq), (wo_hbm, wo))
        )
    ]
    for load in loads:
        load.start()

    barrier = pltpu.get_barrier_semaphore()

    def greet(step, carry):
        pl.semaphore_signal(
            barrier, inc=1, device_id={"seq": (me + step) % SEQ}, device_id_type=MESH
        )
        return carry

    lax.fori_loop(1, SEQ, greet, 0)
    up, down = (z + 1) % RING, (z + RING - 1) % RING
    for neighbour in (up, down):
        pl.semaphore_signal(barrier, inc=1, device_id={"head": neighbour}, device_id_type=MESH)

    averages = coarse_matrix()
    loads[0].wait()
    loads[1].wait()
    key = dot(tok[...], wk[...]).astype(BF16)
    loads[2].wait()
    value = dot(tok[...], wv[...]).astype(BF16)
    coarse_key = dot(averages, key)
    coarse_value = dot(averages, value)
    start = 0
    for level in range(1, LEVELS + 1):
        count = ROWS >> level
        rows = slice(start, start + count)
        sends[level - 1][...] = jnp.concatenate(
            [coarse_key[rows], coarse_value[rows]], axis=0
        ).astype(BF16)
        start += count

    pl.semaphore_wait(barrier, SEQ - 1 + 2)

    for level in range(LEVELS, 0, -1):
        many = 1 << (level - 1)
        first = ((me // many) ^ 1) * many
        slot = me % many

        def post(step, carry, level=level, many=many, first=first, slot=slot):
            pltpu.make_async_remote_copy(
                src_ref=sends[level - 1],
                dst_ref=lands[level - 1].at[slot],
                send_sem=send_sem.at[level - 1],
                recv_sem=recv_sem.at[level - 1],
                device_id={"seq": first + (step + slot) % many},
                device_id_type=MESH,
            ).start()
            return carry

        lax.fori_loop(0, many, post, 0)

    loads[3].wait()
    query = dot(tok[...], wq[...]).astype(BF16)
    fine = []
    for level in range(1, LEVELS + 1):
        wide = dot(averaging_rows(level), query)
        high = wide.astype(BF16)
        low = (wide - high.astype(F32)).astype(BF16)
        fine.append((high, low))

    states = []
    for head in range(2):
        cols = slice(head * HEAD_DIM, (head + 1) * HEAD_DIM)
        scores = dot_nt(query[:, cols], key[:, cols]) * SCORE_SCALE
        top = jnp.max(scores, axis=1, keepdims=True)
        weights = jnp.exp2(scores - top)
        total = jnp.sum(weights, axis=1, keepdims=True)
        states.append((top, total, dot(weights.astype(BF16), value[:, cols])))

    far_keys, far_values = [], []
    for level in range(1, LEVELS + 1):
        many = 1 << (level - 1)
        count = ROWS >> level
        pltpu.make_async_copy(lands[level - 1], lands[level - 1], recv_sem.at[level - 1]).wait()
        if count >= 16:
            block = lands[level - 1][...]
        else:
            block = lands[level - 1][...].astype(F32)
        far_keys.append(block[:, :count, :].reshape(many * count, WIDTH).astype(BF16))
        far_values.append(block[:, count:, :].reshape(many * count, WIDTH).astype(BF16))

    mixed = []
    for head in range(2):
        cols = slice(head * HEAD_DIM, (head + 1) * HEAD_DIM)
        parts = []
        for level in range(1, LEVELS + 1):
            high, low = fine[level - 1]
            left = jnp.concatenate([high[:, cols], low[:, cols]], axis=1)
            right = far_keys[level - 1][:, cols]
            right = jnp.concatenate([right, right], axis=1)
            parts.append(dot_nt(left, right) * SCORE_SCALE + float(level))
        scores = jnp.concatenate(parts, axis=1)
        top, total, summed = states[head]
        newest = jnp.maximum(top, jnp.max(scores, axis=1, keepdims=True))
        old = jnp.exp2(top - newest)
        weights = jnp.exp2(scores - newest)
        values = jnp.concatenate([block[:, cols] for block in far_values], axis=0)
        total = total * old + jnp.sum(weights, axis=1, keepdims=True)
        summed = summed * old + dot(weights.astype(BF16), values)
        mixed.append((summed / total).astype(BF16))
    attention = jnp.concatenate(mixed, axis=1)

    loads[4].wait()

    def hop(way, chain, number):
        index = way * 7 + (number if chain == 0 else 4 + number)
        return pltpu.make_async_remote_copy(
            src_ref=stage.at[index],
            dst_ref=ring.at[index],
            send_sem=ring_send.at[index],
            recv_sem=ring_recv.at[index],
            device_id={"head": up if way == 0 else down},
            device_id_type=MESH,
        ), index

    def own(way, chain, distance):
        half = way if chain == 0 else 1 - way
        target = (z + distance) % RING if way == 0 else (z + RING - distance) % RING
        first = pl.multiple_of(target * PIECE, PIECE)
        return partial[pl.ds(first, PIECE), half * HALF:(half + 1) * HALF]

    hops = []

    def send(way, chain, number):
        copy, index = hop(way, chain, number)
        distance = 4 - number if chain == 0 else 3 - number
        term = own(way, chain, distance)
        if number > 0:
            before, previous = hop(way, chain, number - 1)
            before.wait_recv()
            term = term + ring[previous].astype(F32)
        stage[index] = term.astype(BF16)
        copy.start()
        hops.append(copy)

    for half in range(2):
        columns = slice(half * HALF, (half + 1) * HALF)
        partial[:, columns] = dot(attention, wo[:, columns])
        send(half, 0, 0)
    for way in range(2):
        send(way, 1, 0)
    for number in range(1, 4):
        for chain in range(2):
            if chain == 1 and number == 3:
                continue
            for way in range(2):
                send(way, chain, number)
    mine = pl.multiple_of(z * PIECE, PIECE)
    for half in range(2):
        other = 1 - half
        short, short_index = hop(other, 1, 2)
        long, long_index = hop(half, 0, 3)
        short.wait_recv()
        total = partial[pl.ds(mine, PIECE), half * HALF:(half + 1) * HALF]
        total = total + ring[short_index].astype(F32)
        long.wait_recv()
        total = total + ring[long_index].astype(F32)
        out_ref[:, half * HALF:(half + 1) * HALF] = total.astype(BF16)

    for copy in hops:
        copy.wait_send()
    for level in range(1, LEVELS + 1):
        pltpu.make_async_copy(lands[level - 1], lands[level - 1], send_sem.at[level - 1]).wait()


def shards(tokens, w_query, w_key, w_value, w_out):
    message = [(2 * (ROWS >> level), WIDTH) for level in range(1, LEVELS + 1)]
    return pl.pallas_call(
        kernel,
        out_shape=jax.ShapeDtypeStruct((PIECE, MODEL), BF16),
        in_specs=[pl.BlockSpec(memory_space=pl.ANY)] * 5,
        out_specs=pl.BlockSpec(memory_space=pltpu.VMEM),
        scratch_shapes=[
            pltpu.VMEM((ROWS, MODEL), BF16),
            pltpu.VMEM((MODEL, WIDTH), BF16),
            pltpu.VMEM((MODEL, WIDTH), BF16),
            pltpu.VMEM((MODEL, WIDTH), BF16),
            pltpu.VMEM((WIDTH, MODEL), BF16),
            *[pltpu.VMEM(shape, BF16) for shape in message],
            *[pltpu.VMEM((1 << i, *shape), BF16) for i, shape in enumerate(message)],
            pltpu.VMEM((ROWS, MODEL), F32),
            pltpu.VMEM((14, PIECE, HALF), BF16),
            pltpu.VMEM((14, PIECE, HALF), BF16),
            pltpu.SemaphoreType.DMA((5,)),
            pltpu.SemaphoreType.DMA((LEVELS,)),
            pltpu.SemaphoreType.DMA((LEVELS,)),
            pltpu.SemaphoreType.DMA((14,)),
            pltpu.SemaphoreType.DMA((14,)),
        ],
        compiler_params=pltpu.CompilerParams(
            collective_id=0, has_side_effects=True, vmem_limit_bytes=40 * 1024 * 1024
        ),
    )(tokens, w_query, w_key, w_value, w_out)


def solution(mesh):
    placed = (P("seq", None), P(None, "head"), P(None, "head"), P(None, "head"), P("head", None))
    return jax.shard_map(
        shards, mesh=mesh, in_specs=placed, out_specs=P(("seq", "head"), None), check_vma=False
    )
```

time: 109 us -> 43.2 us (0.40)
  waiting for transfers between devices: 46.6 us -> 0 us
  Pallas kernels: 0 us -> 36.1 us
  starting transfers between devices: 15.7 us -> 0 us
  between operations: 14.1 us -> 0.01 us
  matrix products: 12.7 us -> 0 us
  other arithmetic: 7.08 us -> 0 us
  local copies, waits for them, and re-layouts: 12.6 us -> 6.78 us
    reduce_scatter x1 -> x0, waiting for transfers between devices: 40.6 us -> none  [shards(): lax.psum_scatter(jnp.dot(attention, w_out, preferred_element_type=jnp.flo...]
    pallas_call x0 -> x1, Pallas kernels: none -> 36.1 us  [shards(): pl.pallas_call(kernel, out_shape=jax.ShapeDtypeStruct((PIECE, MODEL), BF1...]
    ppermute x10 -> x0, starting transfers between devices: 15.7 us -> none  [swapped(): return lax.ppermute(block, axis, route)]
    dot_general x16 -> x0, matrix products: 12.7 us -> none  [the longest x3 6.02 us: project(): jnp.dot(tokens, weight, preferred_element_type=jnp.float32)]
    ppermute x10 -> x0, waiting for transfers between devices: 6.05 us -> none  [swapped(): return lax.ppermute(block, axis, route)]
    unnamed x14 -> x11, local copies, waits for them, and re-layouts: 1.07 us -> 6.78 us
    reduce_sum x20 -> x0, other arithmetic: 4.4 us -> none  [the longest x14 3.43 us: coarsen(): wide.reshape((wide.shape[0] // factor, factor) + wide.shape[1:])]
    mul x10 -> x0, local copies, waits for them, and re-layouts: 3.35 us -> none  [merge_level(): summed = state[2] * old_factor[..., None] + part[2] * new_factor[..., None]]
  transfers between devices with their start and end apart: 11 -> 0, of which waited for: 6 -> 0; matrix products, arithmetic and copies ran while one was open for 19% -> 0% of each run, Pallas kernels for 0% -> 0%
where the time goes in v1:
time: 43.2 us; the launch traced here: 42.9 us
  Pallas kernels  36.1 us (84%)
  local copies, waits for them, and re-layouts  6.78 us (16%)
    pallas_call x1, Pallas kernels, shards(): pl.pallas_call(kernel, out_shape=jax.ShapeDtypeStruct((PIECE, MODEL), BF1...  36.1 us
    unnamed x11, local copies, waits for them, and re-layouts  6.78 us

profile of v1, /device:TPU:2, one launch (start us, length us, event | category | flops | bytes accessed | tf_op | source)
XLA Modules:
  0.0 42.9 jit_solution(18208822997932613212)
XLA Ops:
  0.0 0.0 copy-start
  0.0 1.2 %copy-done = bf16[256,2048]{1,0:T(8,128)(2,1)S(1)} copy-done((bf16[256,2048]{1,0:T(8,128)(2,1)S(1)}, bf16[256,2048]{1,0:T(8,128)(2,1)}, u32[]{:S(2)}) %copy-start) | copy-done | bytes 1048600
  1.2 0.0 copy-start.1
  1.2 1.2 %copy-done.1 = bf16[2048,256]{1,0:T(8,128)(2,1)S(1)} copy-done((bf16[2048,256]{1,0:T(8,128)(2,1)S(1)}, bf16[2048,256]{1,0:T(8,128)(2,1)}, u32[]{:S(2)}) %copy-start.1) | copy-done | bytes 1048600
  2.5 0.0 copy-start.2
  2.5 1.2 %copy-done.2 = bf16[2048,256]{1,0:T(8,128)(2,1)S(1)} copy-done((bf16[2048,256]{1,0:T(8,128)(2,1)S(1)}, bf16[2048,256]{1,0:T(8,128)(2,1)}, u32[]{:S(2)}) %copy-start.2) | copy-done | bytes 1048600
  3.7 0.0 copy-start.3
  3.7 1.2 %copy-done.3 = bf16[2048,256]{1,0:T(8,128)(2,1)S(1)} copy-done((bf16[2048,256]{1,0:T(8,128)(2,1)S(1)}, bf16[2048,256]{1,0:T(8,128)(2,1)}, u32[]{:S(2)}) %copy-start.3) | copy-done | bytes 1048600
  4.9 0.0 copy-start.4
  4.9 1.2 %copy-done.4 = bf16[256,2048]{1,0:T(8,128)(2,1)S(1)} copy-done((bf16[256,2048]{1,0:T(8,128)(2,1)S(1)}, bf16[256,2048]{1,0:T(8,128)(2,1)}, u32[]{:S(2)}) %copy-start.4) | copy-done | bytes 1048600
  6.1 36.1 %shard_map.55 = bf16[32,2048]{1,0:T(8,128)(2,1)S(1)} custom-call(bf16[256,2048]{1,0:T(8,128)(2,1)S(1)} %copy-done, bf16[2048,256]{1,0:T(8,128)(2,1)S(1)} %copy-done.1, bf16[2048,256]{1,0:T(8,128)(2,1)S(1)} %copy-done.2, bf16[2048,256]{1,0:T(8,128)(2,1)S(1)} %copy-done.3, bf16[256,2048]{1,0:T(8,128)(2,1)S(1)} %copy-done.4), custom_call_target="tpu_custom_call" | custom-call | tf_op jit(solution)/shard_map/pallas_call | solution.py:243
  42.2 0.7 %copy.7 = bf16[32,2048]{1,0:T(8,128)(2,1)} copy(bf16[32,2048]{1,0:T(8,128)(2,1)S(1)} %shard_map.55) | data formatting | bytes 262144
Async XLA Ops:
  0.0 1.2 %copy-start = (bf16[256,2048]{1,0:T(8,128)(2,1)S(1)}, bf16[256,2048]{1,0:T(8,128)(2,1)}, u32[]{:S(2)}) copy-start(bf16[256,2048]{1,0:T(8,128)(2,1)} %tok_hbm.1) | copy-start | bytes 3145732
  1.2 1.2 %copy-start.1 = (bf16[2048,256]{1,0:T(8,128)(2,1)S(1)}, bf16[2048,256]{1,0:T(8,128)(2,1)}, u32[]{:S(2)}) copy-start(bf16[2048,256]{1,0:T(8,128)(2,1)} %wq_hbm.1) | copy-start | bytes 3145732
  2.5 1.2 %copy-start.2 = (bf16[2048,256]{1,0:T(8,128)(2,1)S(1)}, bf16[2048,256]{1,0:T(8,128)(2,1)}, u32[]{:S(2)}) copy-start(bf16[2048,256]{1,0:T(8,128)(2,1)} %wk_hbm.1) | copy-start | bytes 3145732
  3.7 1.2 %copy-start.3 = (bf16[2048,256]{1,0:T(8,128)(2,1)S(1)}, bf16[2048,256]{1,0:T(8,128)(2,1)}, u32[]{:S(2)}) copy-start(bf16[2048,256]{1,0:T(8,128)(2,1)} %wv_hbm.1) | copy-start | bytes 3145732
  4.9 1.2 %copy-start.4 = (bf16[256,2048]{1,0:T(8,128)(2,1)S(1)}, bf16[256,2048]{1,0:T(8,128)(2,1)}, u32[]{:S(2)}) copy-start(bf16[256,2048]{1,0:T(8,128)(2,1)} %wo_hbm.1) | copy-start | bytes 3145732

commit v2 on v1

v2 whole, which is shorter than its diff:
```python
import functools
import math

import jax
import jax.numpy as jnp
from jax import lax
from jax.experimental import pallas as pl
from jax.experimental.pallas import tpu as pltpu
from jax.sharding import PartitionSpec as P

HEAD_DIM = 128
ROWS = 256
WIDTH = 256
MODEL = 2048
HALF = MODEL // 2
PARTS = 1
COLS = HALF // PARTS
LEVELS = 5
FAR = LEVELS * HEAD_DIM
ORDER = (5, 4, 3, 2, 1)
FORWARD = (2, 3, 4, 5,)
SEQ = 32
RING = 8
PIECE = ROWS // RING
LOG2_E = 1.4426950408889634
SCORE_SCALE = LOG2_E / math.sqrt(HEAD_DIM)
MESH = pl.DeviceIdType.MESH
BF16 = jnp.bfloat16
F32 = jnp.float32
VMEM_BYTES = 107 * 512 * 1024


def dot(a, b):
    return jnp.dot(a, b, preferred_element_type=F32)


def dot_nt(a, b):
    return lax.dot_general(a, b, (((1,), (1,)), ((), ())), preferred_element_type=F32)


def averaging_rows(level):
    row = lax.broadcasted_iota(jnp.int32, (ROWS, ROWS), 0)
    col = lax.broadcasted_iota(jnp.int32, (ROWS, ROWS), 1)
    same = (row >> level) == (col >> level)
    return jnp.where(same, 2.0**-level, 0.0).astype(BF16)


def coarse_matrix():
    row = lax.broadcasted_iota(jnp.int32, (ROWS, ROWS), 0)
    col = lax.broadcasted_iota(jnp.int32, (ROWS, ROWS), 1)
    total = jnp.zeros((ROWS, ROWS), F32)
    start = 0
    for level in range(1, LEVELS + 1):
        count = ROWS >> level
        hit = (row >= start) & (row < start + count) & ((col >> level) == row - start)
        total = jnp.where(hit, 2.0**-level, total)
        start += count
    return total.astype(BF16)


def kernel(
    tok_hbm, wq_hbm, wk_hbm, wv_hbm, wo_hbm, out_ref,
    tok, wq, wk, wv, wo,
    send1, send2, send3, send4, send5,
    land1, land2, land3, land4, land5,
    fine, near_top, near_total, near_sum, far_key, far_value,
    partial, stage, ring,
    load_sem, send_sem, recv_sem, pass_send, pass_recv, ring_send, ring_recv,
):
    sends = (send1, send2, send3, send4, send5)
    lands = (land1, land2, land3, land4, land5)
    me = lax.axis_index("seq")
    z = lax.axis_index("head")
    core = me % 2

    loads = [
        pltpu.make_async_copy(src, dst, load_sem.at[i])
        for i, (src, dst) in enumerate(
            ((tok_hbm, tok), (wk_hbm, wk), (wv_hbm, wv), (wq_hbm, wq), (wo_hbm, wo))
        )
    ]
    for load in loads:
        load.start()

    barrier = pltpu.get_barrier_semaphore()

    def greet(step, carry):
        pl.semaphore_signal(
            barrier, inc=1, device_id={"seq": (me + step) % SEQ}, device_id_type=MESH
        )
        return carry

    lax.fori_loop(1, SEQ, greet, 0)
    up, down = (z + 1) % RING, (z + RING - 1) % RING
    for neighbour in (up, down):
        pl.semaphore_signal(barrier, inc=1, device_id={"head": neighbour}, device_id_type=MESH)

    averages = coarse_matrix()
    loads[0].wait()
    loads[1].wait()
    key = dot(tok[...], wk[...]).astype(BF16)
    loads[2].wait()
    value = dot(tok[...], wv[...]).astype(BF16)
    coarse_key = dot(averages, key)
    coarse_value = dot(averages, value)
    start = 0
    for level in range(1, LEVELS + 1):
        count = ROWS >> level
        rows = slice(start, start + count)
        sends[level - 1][...] = jnp.concatenate(
            [coarse_key[rows], coarse_value[rows]], axis=0
        ).astype(BF16)
        start += count

    pl.semaphore_wait(barrier, SEQ - 1 + 2)

    for level in ORDER:
        many = 1 << (level - 1)
        first = ((me // many) ^ 1) * many
        place = me % many
        slot = place if level == 1 else core * (many // 2) + place // 2
        step_of = 2 if level in FORWARD else 1

        def post(step, carry, level=level, many=many, first=first, place=place, slot=slot, by=step_of):
            pltpu.make_async_remote_copy(
                src_ref=sends[level - 1],
                dst_ref=lands[level - 1].at[slot],
                send_sem=send_sem.at[level - 1],
                recv_sem=recv_sem.at[level - 1],
                device_id={"seq": first + (by * step + place) % many},
                device_id_type=MESH,
            ).start()
            return carry

        lax.fori_loop(0, many // step_of, post, 0)

    loads[3].wait()
    query = dot(tok[...], wq[...]).astype(BF16)
    for level in range(1, LEVELS + 1):
        wide = dot(averaging_rows(level), query)
        high = wide.astype(BF16)
        low = (wide - high.astype(F32)).astype(BF16)
        for head in range(2):
            cols = slice(head * HEAD_DIM, (head + 1) * HEAD_DIM)
            fine[level - 1, head, :, :HEAD_DIM] = high[:, cols]
            fine[level - 1, head, :, HEAD_DIM:] = low[:, cols]

    for head in range(2):
        cols = slice(head * HEAD_DIM, (head + 1) * HEAD_DIM)
        scores = dot_nt(query[:, cols], key[:, cols]) * SCORE_SCALE
        top = jnp.max(scores, axis=1, keepdims=True)
        weights = jnp.exp2(scores - top)
        total = jnp.sum(weights, axis=1, keepdims=True)
        near_top[head] = jnp.broadcast_to(top, (ROWS, HEAD_DIM))
        near_total[head] = jnp.broadcast_to(total, (ROWS, HEAD_DIM))
        near_sum[head] = dot(weights.astype(BF16), value[:, cols])

    def received(level):
        return lands[level - 1].at[pl.ds(core * (1 << (level - 2)), 1 << (level - 2))]

    def passed(level):
        return lands[level - 1].at[pl.ds((1 - core) * (1 << (level - 2)), 1 << (level - 2))]

    def handover(level):
        return pltpu.make_async_remote_copy(
            src_ref=received(level),
            dst_ref=received(level),
            send_sem=pass_send.at[level - 1],
            recv_sem=pass_recv.at[level - 1],
            device_id={"seq": me ^ 1},
            device_id_type=MESH,
        )

    for level in FORWARD:
        pltpu.make_async_copy(received(level), received(level), recv_sem.at[level - 1]).wait()
        handover(level).start()

    for level in range(1, LEVELS + 1):
        many = 1 << (level - 1)
        count = ROWS >> level
        if level in FORWARD:
            pltpu.make_async_copy(passed(level), passed(level), pass_recv.at[level - 1]).wait()
        else:
            pltpu.make_async_copy(lands[level - 1], lands[level - 1], recv_sem.at[level - 1]).wait()
        block = lands[level - 1][...]
        if count < 16:
            block = block.astype(F32)
        keys = block[:, :count, :].reshape(many * count, WIDTH).astype(BF16)
        values = block[:, count:, :].reshape(many * count, WIDTH).astype(BF16)
        rows = slice((level - 1) * HEAD_DIM, level * HEAD_DIM)
        for head in range(2):
            cols = slice(head * HEAD_DIM, (head + 1) * HEAD_DIM)
            far_key[head, rows, :HEAD_DIM] = keys[:, cols]
            far_key[head, rows, HEAD_DIM:] = keys[:, cols]
            far_value[head, rows, :] = values[:, cols]

    def attend(rows):
        mixed = []
        for head in range(2):
            parts = []
            for level in range(1, LEVELS + 1):
                section = slice((level - 1) * HEAD_DIM, level * HEAD_DIM)
                product = dot_nt(fine[level - 1, head, rows, :], far_key[head, section, :])
                parts.append(product * SCORE_SCALE + float(level))
            scores = jnp.concatenate(parts, axis=1)
            top = near_top[head, rows, :][:, :1]
            newest = jnp.maximum(top, jnp.max(scores, axis=1, keepdims=True))
            old = jnp.exp2(top - newest)
            weights = jnp.exp2(scores - newest)
            total = near_total[head, rows, :][:, :1] * old + jnp.sum(weights, axis=1, keepdims=True)
            summed = near_sum[head, rows, :] * old + dot(weights.astype(BF16), far_value[head])
            mixed.append((summed / total).astype(BF16))
        return jnp.concatenate(mixed, axis=1)

    def hop(way, chain, part, number):
        index = (way * 7 + (number if chain == 0 else 4 + number)) * PARTS + part
        return pltpu.make_async_remote_copy(
            src_ref=stage.at[index],
            dst_ref=ring.at[index],
            send_sem=ring_send.at[index],
            recv_sem=ring_recv.at[index],
            device_id={"head": up if way == 0 else down},
            device_id_type=MESH,
        ), index

    def columns_of(half, part):
        first = half * HALF + part * COLS
        return slice(first, first + COLS)

    def own(way, chain, part, distance):
        half = way if chain == 0 else 1 - way
        target = (z + distance) % RING if way == 0 else (z + RING - distance) % RING
        first = pl.multiple_of(target * PIECE, PIECE)
        return partial[pl.ds(first, PIECE), columns_of(half, part)]

    hops = []

    def send(way, chain, part, number):
        copy, index = hop(way, chain, part, number)
        term = own(way, chain, part, 4 - number if chain == 0 else 3 - number)
        if number > 0:
            before, previous = hop(way, chain, part, number - 1)
            before.wait_recv()
            term = term + ring[previous].astype(F32)
        stage[index] = term.astype(BF16)
        copy.start()
        hops.append(copy)

    loads[4].wait()
    opposite = pl.ds(pl.multiple_of(((z + RING // 2) % RING) * PIECE, PIECE), PIECE)
    attention = attend(opposite)
    for part in range(PARTS):
        for way in range(2):
            copy, index = hop(way, 0, part, 0)
            stage[index] = dot(attention, wo[:, columns_of(way, part)]).astype(BF16)
            copy.start()
            hops.append(copy)

    partial[...] = dot(attend(slice(0, ROWS)), wo[...])
    for part in range(PARTS):
        for way in range(2):
            send(way, 1, part, 0)
    for number in range(1, 4):
        for chain in range(2):
            if chain == 1 and number == 3:
                continue
            for part in range(PARTS):
                for way in range(2):
                    send(way, chain, part, number)
    mine = pl.multiple_of(z * PIECE, PIECE)
    for part in range(PARTS):
        for half in range(2):
            columns = columns_of(half, part)
            short, short_index = hop(1 - half, 1, part, 2)
            long, long_index = hop(half, 0, part, 3)
            short.wait_recv()
            total = partial[pl.ds(mine, PIECE), columns]
            total = total + ring[short_index].astype(F32)
            long.wait_recv()
            total = total + ring[long_index].astype(F32)
            out_ref[:, columns] = total.astype(BF16)

    for copy in hops:
        copy.wait_send()
    for level in range(1, LEVELS + 1):
        if level in FORWARD:
            handover(level).wait_send()
            pltpu.make_async_copy(received(level), received(level), send_sem.at[level - 1]).wait()
        else:
            pltpu.make_async_copy(lands[level - 1], lands[level - 1], send_sem.at[level - 1]).wait()


def shards(tokens, w_query, w_key, w_value, w_out):
    message = [(2 * (ROWS >> level), WIDTH) for level in range(1, LEVELS + 1)]
    return pl.pallas_call(
        kernel,
        out_shape=jax.ShapeDtypeStruct((PIECE, MODEL), BF16),
        in_specs=[pl.BlockSpec(memory_space=pl.ANY)] * 5,
        out_specs=pl.BlockSpec(memory_space=pltpu.VMEM),
        scratch_shapes=[
            pltpu.VMEM((ROWS, MODEL), BF16),
            pltpu.VMEM((MODEL, WIDTH), BF16),
            pltpu.VMEM((MODEL, WIDTH), BF16),
            pltpu.VMEM((MODEL, WIDTH), BF16),
            pltpu.VMEM((WIDTH, MODEL), BF16),
            *[pltpu.VMEM(shape, BF16) for shape in message],
            *[pltpu.VMEM((1 << i, *shape), BF16) for i, shape in enumerate(message)],
            pltpu.VMEM((LEVELS, 2, ROWS, 2 * HEAD_DIM), BF16),
            pltpu.VMEM((2, ROWS, HEAD_DIM), F32),
            pltpu.VMEM((2, ROWS, HEAD_DIM), F32),
            pltpu.VMEM((2, ROWS, HEAD_DIM), F32),
            pltpu.VMEM((2, FAR, 2 * HEAD_DIM), BF16),
            pltpu.VMEM((2, FAR, HEAD_DIM), BF16),
            pltpu.VMEM((ROWS, MODEL), F32),
            pltpu.VMEM((14 * PARTS, PIECE, COLS), BF16),
            pltpu.VMEM((14 * PARTS, PIECE, COLS), BF16),
            pltpu.SemaphoreType.DMA((5,)),
            pltpu.SemaphoreType.DMA((LEVELS,)),
            pltpu.SemaphoreType.DMA((LEVELS,)),
            pltpu.SemaphoreType.DMA((LEVELS,)),
            pltpu.SemaphoreType.DMA((LEVELS,)),
            pltpu.SemaphoreType.DMA((14 * PARTS,)),
            pltpu.SemaphoreType.DMA((14 * PARTS,)),
        ],
        compiler_params=pltpu.CompilerParams(
            collective_id=0, has_side_effects=True, vmem_limit_bytes=VMEM_BYTES
        ),
    )(tokens, w_query, w_key, w_value, w_out)


def solution(mesh):
    placed = (P("seq", None), P(None, "head"), P(None, "head"), P(None, "head"), P("head", None))
    return jax.shard_map(
        shards, mesh=mesh, in_specs=placed, out_specs=P(("seq", "head"), None), check_vma=False
    )
```

time: 43.2 us -> 33.1 us (0.77)
  local copies, waits for them, and re-layouts: 6.78 us -> 0.66 us
  Pallas kernels: 36.1 us -> 32 us
    unnamed x11 -> x1, local copies, waits for them, and re-layouts: 6.78 us -> 0.66 us
    pallas_call x1, Pallas kernels: 36.1 us -> 32 us  [shards(): pl.pallas_call(kernel, out_shape=jax.ShapeDtypeStruct((PIECE, MODEL), BF1...]
where the time goes in v2:
time: 33.1 us; the launch traced here: 32.7 us
  Pallas kernels  32 us (97%)
  local copies, waits for them, and re-layouts  0.66 us (2%)
    pallas_call x1, Pallas kernels, shards(): pl.pallas_call(kernel, out_shape=jax.ShapeDtypeStruct((PIECE, MODEL), BF1...  32 us

profile of v2, /device:TPU:2, one launch (start us, length us, event | category | flops | bytes accessed | tf_op | source)
XLA Modules:
  0.0 32.7 jit_solution(12451684478721631817)
XLA Ops:
  0.0 32.0 %shard_map.55 = bf16[32,2048]{1,0:T(8,128)(2,1)S(1)} custom-call(bf16[256,2048]{1,0:T(8,128)(2,1)} %tok_hbm.1, bf16[2048,256]{1,0:T(8,128)(2,1)} %wq_hbm.1, bf16[2048,256]{1,0:T(8,128)(2,1)} %wk_hbm.1, bf16[2048,256]{1,0:T(8,128)(2,1)} %wv_hbm.1, bf16[256,2048]{1,0:T(8,128)(2,1)} %wo_hbm.1), custom_call_target="tpu_custom_call" | custom-call | tf_op jit(solution)/shard_map/pallas_call | solution.py:295
  32.0 0.7 %copy.7 = bf16[32,2048]{1,0:T(8,128)(2,1)} copy(bf16[32,2048]{1,0:T(8,128)(2,1)S(1)} %shard_map.55) | data formatting | bytes 262144

commit v3 on v2

--- a/solution.py
+++ b/solution.py
@@ -73,6 +73,19 @@
     z = lax.axis_index("head")
     core = me % 2
 
+    barrier = pltpu.get_barrier_semaphore()
+
+    def greet(step, carry):
+        pl.semaphore_signal(
+            barrier, inc=1, device_id={"seq": (me + step) % SEQ}, device_id_type=MESH
+        )
+        return carry
+
+    lax.fori_loop(1, SEQ, greet, 0)
+    up, down = (z + 1) % RING, (z + RING - 1) % RING
+    for neighbour in (up, down):
+        pl.semaphore_signal(barrier, inc=1, device_id={"head": neighbour}, device_id_type=MESH)
+
     loads = [
         pltpu.make_async_copy(src, dst, load_sem.at[i])
         for i, (src, dst) in enumerate(
@@ -81,19 +94,6 @@
     ]
     for load in loads:
         load.start()
-
-    barrier = pltpu.get_barrier_semaphore()
-
-    def greet(step, carry):
-        pl.semaphore_signal(
-            barrier, inc=1, device_id={"seq": (me + step) % SEQ}, device_id_type=MESH
-        )
-        return carry
-
-    lax.fori_loop(1, SEQ, greet, 0)
-    up, down = (z + 1) % RING, (z + RING - 1) % RING
-    for neighbour in (up, down):
-        pl.semaphore_signal(barrier, inc=1, device_id={"head": neighbour}, device_id_type=MESH)
 
     averages = coarse_matrix()
     loads[0].wait()
@@ -171,28 +171,31 @@
             device_id_type=MESH,
         )
 
-    for level in FORWARD:
-        pltpu.make_async_copy(received(level), received(level), recv_sem.at[level - 1]).wait()
-        handover(level).start()
-
-    for level in range(1, LEVELS + 1):
-        many = 1 << (level - 1)
+    def take(level, slots, place):
         count = ROWS >> level
-        if level in FORWARD:
-            pltpu.make_async_copy(passed(level), passed(level), pass_recv.at[level - 1]).wait()
-        else:
-            pltpu.make_async_copy(lands[level - 1], lands[level - 1], recv_sem.at[level - 1]).wait()
-        block = lands[level - 1][...]
+        block = lands[level - 1][slots]
         if count < 16:
             block = block.astype(F32)
-        keys = block[:, :count, :].reshape(many * count, WIDTH).astype(BF16)
-        values = block[:, count:, :].reshape(many * count, WIDTH).astype(BF16)
-        rows = slice((level - 1) * HEAD_DIM, level * HEAD_DIM)
+        length = block.shape[0] * count
+        keys = block[:, :count, :].reshape(length, WIDTH).astype(BF16)
+        values = block[:, count:, :].reshape(length, WIDTH).astype(BF16)
+        rows = slice((level - 1) * HEAD_DIM + place, (level - 1) * HEAD_DIM + place + length)
         for head in range(2):
             cols = slice(head * HEAD_DIM, (head + 1) * HEAD_DIM)
             far_key[head, rows, :HEAD_DIM] = keys[:, cols]
             far_key[head, rows, HEAD_DIM:] = keys[:, cols]
             far_value[head, rows, :] = values[:, cols]
+
+    for level in (4, 5, 3, 2):
+        pltpu.make_async_copy(received(level), received(level), recv_sem.at[level - 1]).wait()
+        handover(level).start()
+    pltpu.make_async_copy(land1, land1, recv_sem.at[0]).wait()
+    take(1, slice(0, 1), 0)
+    for level in FORWARD:
+        take(level, pl.ds(core * (1 << (level - 2)), 1 << (level - 2)), 0)
+    for level in (4, 5, 3, 2):
+        pltpu.make_async_copy(passed(level), passed(level), pass_recv.at[level - 1]).wait()
+        take(level, pl.ds((1 - core) * (1 << (level - 2)), 1 << (level - 2)), HEAD_DIM // 2)
 
     def attend(rows):
         mixed = []

time: 33.1 us -> 32.6 us (0.985)
  Pallas kernels: 32 us -> 31.6 us
    pallas_call x1, Pallas kernels: 32 us -> 31.6 us  [shards(): pl.pallas_call(kernel, out_shape=jax.ShapeDtypeStruct((PIECE, MODEL), BF1...]
where the time goes in v3:
time: 32.6 us; the launch traced here: 32.3 us
  Pallas kernels  31.6 us (97%)
  local copies, waits for them, and re-layouts  0.66 us (2%)
    pallas_call x1, Pallas kernels, shards(): pl.pallas_call(kernel, out_shape=jax.ShapeDtypeStruct((PIECE, MODEL), BF1...  31.6 us
    unnamed x1, local copies, waits for them, and re-layouts  0.66 us

profile of v3, /device:TPU:2, one launch (start us, length us, event | category | flops | bytes accessed | tf_op | source)
XLA Modules:
  0.0 32.3 jit_solution(14076102333290158917)
XLA Ops:
  0.0 31.6 %shard_map.55 = bf16[32,2048]{1,0:T(8,128)(2,1)S(1)} custom-call(bf16[256,2048]{1,0:T(8,128)(2,1)} %tok_hbm.1, bf16[2048,256]{1,0:T(8,128)(2,1)} %wq_hbm.1, bf16[2048,256]{1,0:T(8,128)(2,1)} %wk_hbm.1, bf16[2048,256]{1,0:T(8,128)(2,1)} %wv_hbm.1, bf16[256,2048]{1,0:T(8,128)(2,1)} %wo_hbm.1), custom_call_target="tpu_custom_call" | custom-call | tf_op jit(solution)/shard_map/pallas_call | solution.py:298
  31.6 0.7 %copy.7 = bf16[32,2048]{1,0:T(8,128)(2,1)} copy(bf16[32,2048]{1,0:T(8,128)(2,1)S(1)} %shard_map.55) | data formatting | bytes 262144

commit v4 on v3

--- a/solution.py
+++ b/solution.py
@@ -19,6 +19,8 @@
 FAR = LEVELS * HEAD_DIM
 ORDER = (5, 4, 3, 2, 1)
 FORWARD = (2, 3, 4, 5,)
+CHUNKS = 4
+DEPTH = MODEL // CHUNKS
 SEQ = 32
 RING = 8
 PIECE = ROWS // RING
@@ -77,30 +79,41 @@
 
     def greet(step, carry):
         pl.semaphore_signal(
-            barrier, inc=1, device_id={"seq": (me + step) % SEQ}, device_id_type=MESH
+            barrier, inc=1, device_id={"seq": (me + 2 * step) % SEQ}, device_id_type=MESH
         )
         return carry
 
-    lax.fori_loop(1, SEQ, greet, 0)
+    lax.fori_loop(1, SEQ // 2, greet, 0)
+    pl.semaphore_signal(barrier, inc=1, device_id={"seq": me ^ 1}, device_id_type=MESH)
     up, down = (z + 1) % RING, (z + RING - 1) % RING
     for neighbour in (up, down):
         pl.semaphore_signal(barrier, inc=1, device_id={"head": neighbour}, device_id_type=MESH)
 
-    loads = [
-        pltpu.make_async_copy(src, dst, load_sem.at[i])
-        for i, (src, dst) in enumerate(
-            ((tok_hbm, tok), (wk_hbm, wk), (wv_hbm, wv), (wq_hbm, wq), (wo_hbm, wo))
-        )
-    ]
-    for load in loads:
+    loads = []
+    for c in range(CHUNKS):
+        span = pl.ds(c * DEPTH, DEPTH)
+        for src, dst in (
+            (tok_hbm.at[:, span], tok.at[:, span]),
+            (wk_hbm.at[span], wk.at[span]),
+            (wv_hbm.at[span], wv.at[span]),
+        ):
+            loads.append(pltpu.make_async_copy(src, dst, load_sem.at[len(loads)]))
+    load_query = pltpu.make_async_copy(wq_hbm, wq, load_sem.at[3 * CHUNKS])
+    load_out = pltpu.make_async_copy(wo_hbm, wo, load_sem.at[3 * CHUNKS + 1])
+    for load in (*loads, load_query, load_out):
         load.start()
 
     averages = coarse_matrix()
-    loads[0].wait()
-    loads[1].wait()
-    key = dot(tok[...], wk[...]).astype(BF16)
-    loads[2].wait()
-    value = dot(tok[...], wv[...]).astype(BF16)
+    acc_key = jnp.zeros((ROWS, WIDTH), F32)
+    acc_value = jnp.zeros((ROWS, WIDTH), F32)
+    for c in range(CHUNKS):
+        for load in loads[3 * c:3 * c + 3]:
+            load.wait()
+        span = slice(c * DEPTH, (c + 1) * DEPTH)
+        acc_key += dot(tok[:, span], wk[span, :])
+        acc_value += dot(tok[:, span], wv[span, :])
+    key = acc_key.astype(BF16)
+    value = acc_value.astype(BF16)
     coarse_key = dot(averages, key)
     coarse_value = dot(averages, value)
     start = 0
@@ -112,7 +125,7 @@
         ).astype(BF16)
         start += count
 
-    pl.semaphore_wait(barrier, SEQ - 1 + 2)
+    pl.semaphore_wait(barrier, SEQ // 2 - 1 + 1 + 2)
 
     for level in ORDER:
         many = 1 << (level - 1)
@@ -134,7 +147,7 @@
 
         lax.fori_loop(0, many // step_of, post, 0)
 
-    loads[3].wait()
+    load_query.wait()
     query = dot(tok[...], wq[...]).astype(BF16)
     for level in range(1, LEVELS + 1):
         wide = dot(averaging_rows(level), query)
@@ -249,7 +262,7 @@
         copy.start()
         hops.append(copy)
 
-    loads[4].wait()
+    load_out.wait()
     opposite = pl.ds(pl.multiple_of(((z + RING // 2) % RING) * PIECE, PIECE), PIECE)
     attention = attend(opposite)
     for part in range(PARTS):
@@ -270,20 +283,7 @@
             for part in range(PARTS):
                 for way in range(2):
                     send(way, chain, part, number)
-    mine = pl.multiple_of(z * PIECE, PIECE)
-    for part in range(PARTS):
-        for half in range(2):
-            columns = columns_of(half, part)
-            short, short_index = hop(1 - half, 1, part, 2)
-            long, long_index = hop(half, 0, part, 3)
-            short.wait_recv()
-            total = partial[pl.ds(mine, PIECE), columns]
-            total = total + ring[short_index].astype(F32)
-            long.wait_recv()
-            total = total + ring[long_index].astype(F32)
-            out_ref[:, columns] = total.astype(BF16)
-
-    for copy in hops:
+    for copy in hops[:-4]:
         copy.wait_send()
     for level in range(1, LEVELS + 1):
         if level in FORWARD:
@@ -291,6 +291,20 @@
             pltpu.make_async_copy(received(level), received(level), send_sem.at[level - 1]).wait()
         else:
             pltpu.make_async_copy(lands[level - 1], lands[level - 1], send_sem.at[level - 1]).wait()
+    mine = pl.ds(pl.multiple_of(z * PIECE, PIECE), PIECE)
+    for half in range(2):
+        short, index = hop(1 - half, 1, 0, 2)
+        short.wait_recv()
+        partial[mine, columns_of(half, 0)] += ring[index].astype(F32)
+    for copy in hops[-4:-2]:
+        copy.wait_send()
+    for half in range(2):
+        long, index = hop(half, 0, 0, 3)
+        long.wait_recv()
+        columns = columns_of(half, 0)
+        out_ref[:, columns] = (partial[mine, columns] + ring[index].astype(F32)).astype(BF16)
+    for copy in hops[-2:]:
+        copy.wait_send()
 
 
 def shards(tokens, w_query, w_key, w_value, w_out):
@@ -317,7 +331,7 @@
             pltpu.VMEM((ROWS, MODEL), F32),
             pltpu.VMEM((14 * PARTS, PIECE, COLS), BF16),
             pltpu.VMEM((14 * PARTS, PIECE, COLS), BF16),
-            pltpu.SemaphoreType.DMA((5,)),
+            pltpu.SemaphoreType.DMA((3 * CHUNKS + 2,)),
             pltpu.SemaphoreType.DMA((LEVELS,)),
             pltpu.SemaphoreType.DMA((LEVELS,)),
             pltpu.SemaphoreType.DMA((LEVELS,)),

time: 32.6 us -> 31.6 us (0.969)
  Pallas kernels: 31.6 us -> 30.7 us
    pallas_call x1, Pallas kernels: 31.6 us -> 30.7 us  [shards(): pl.pallas_call(kernel, out_shape=jax.ShapeDtypeStruct((PIECE, MODEL), BF1...]
where the time goes in v4:
time: 31.6 us; the launch traced here: 31.4 us
  Pallas kernels  30.7 us (97%)
  local copies, waits for them, and re-layouts  0.66 us (2%)
    pallas_call x1, Pallas kernels, shards(): pl.pallas_call(kernel, out_shape=jax.ShapeDtypeStruct((PIECE, MODEL), BF1...  30.7 us
    unnamed x1, local copies, waits for them, and re-layouts  0.66 us

profile of v4, /device:TPU:2, one launch (start us, length us, event | category | flops | bytes accessed | tf_op | source)
XLA Modules:
  0.0 31.4 jit_solution(14706559993617818275)
XLA Ops:
  0.0 30.7 %shard_map.55 = bf16[32,2048]{1,0:T(8,128)(2,1)S(1)} custom-call(bf16[256,2048]{1,0:T(8,128)(2,1)} %tok_hbm.1, bf16[2048,256]{1,0:T(8,128)(2,1)} %wq_hbm.1, bf16[2048,256]{1,0:T(8,128)(2,1)} %wk_hbm.1, bf16[2048,256]{1,0:T(8,128)(2,1)} %wv_hbm.1, bf16[256,2048]{1,0:T(8,128)(2,1)} %wo_hbm.1), custom_call_target="tpu_custom_call" | custom-call | tf_op jit(solution)/shard_map/pallas_call | solution.py:312
  30.8 0.7 %copy.7 = bf16[32,2048]{1,0:T(8,128)(2,1)} copy(bf16[32,2048]{1,0:T(8,128)(2,1)S(1)} %shard_map.55) | data formatting | bytes 262144

commit v5 on v4

--- a/solution.py
+++ b/solution.py
@@ -17,6 +17,7 @@
 COLS = HALF // PARTS
 LEVELS = 5
 FAR = LEVELS * HEAD_DIM
+WEIGHTS = tuple(2.0**level for level in range(LEVELS + 1))
 ORDER = (5, 4, 3, 2, 1)
 FORWARD = (2, 3, 4, 5,)
 CHUNKS = 4
@@ -77,6 +78,10 @@
 
     barrier = pltpu.get_barrier_semaphore()
 
+    up, down = (z + 1) % RING, (z + RING - 1) % RING
+    for neighbour in (up, down):
+        pl.semaphore_signal(barrier, inc=1, device_id={"head": neighbour}, device_id_type=MESH)
+
     def greet(step, carry):
         pl.semaphore_signal(
             barrier, inc=1, device_id={"seq": (me + 2 * step) % SEQ}, device_id_type=MESH
@@ -85,10 +90,6 @@
 
     lax.fori_loop(1, SEQ // 2, greet, 0)
     pl.semaphore_signal(barrier, inc=1, device_id={"seq": me ^ 1}, device_id_type=MESH)
-    up, down = (z + 1) % RING, (z + RING - 1) % RING
-    for neighbour in (up, down):
-        pl.semaphore_signal(barrier, inc=1, device_id={"head": neighbour}, device_id_type=MESH)
-
     loads = []
     for c in range(CHUNKS):
         span = pl.ds(c * DEPTH, DEPTH)
@@ -114,20 +115,25 @@
         acc_value += dot(tok[:, span], wv[span, :])
     key = acc_key.astype(BF16)
     value = acc_value.astype(BF16)
-    coarse_key = dot(averages, key)
-    coarse_value = dot(averages, value)
-    start = 0
-    for level in range(1, LEVELS + 1):
-        count = ROWS >> level
-        rows = slice(start, start + count)
-        sends[level - 1][...] = jnp.concatenate(
-            [coarse_key[rows], coarse_value[rows]], axis=0
-        ).astype(BF16)
-        start += count
-
+    def coarsen(levels, start):
+        rows = sum(ROWS >> level for level in levels)
+        matrix = averages[start:start + rows]
+        coarse_key = dot(matrix, key)
+        coarse_value = dot(matrix, value)
+        first = 0
+        for level in levels:
+            section = slice(first, first + (ROWS >> level))
+            sends[level - 1][...] = jnp.concatenate(
+                [coarse_key[section], coarse_value[section]], axis=0
+            ).astype(BF16)
+            first += ROWS >> level
+
+    coarsen((2, 3, 4, 5), HEAD_DIM)
     pl.semaphore_wait(barrier, SEQ // 2 - 1 + 1 + 2)
 
     for level in ORDER:
+        if level == 1:
+            coarsen((1,), 0)
         many = 1 << (level - 1)
         first = ((me // many) ^ 1) * many
         place = me % many
@@ -147,10 +153,15 @@
 
         lax.fori_loop(0, many // step_of, post, 0)
 
+    for level in range(1, LEVELS + 1):
+        rows = slice((level - 1) * HEAD_DIM, level * HEAD_DIM)
+        for head in range(2):
+            far_value[head, rows, HEAD_DIM:] = jnp.full((HEAD_DIM, HEAD_DIM), WEIGHTS[level], BF16)
+
     load_query.wait()
     query = dot(tok[...], wq[...]).astype(BF16)
     for level in range(1, LEVELS + 1):
-        wide = dot(averaging_rows(level), query)
+        wide = dot(averaging_rows(level), query) * SCORE_SCALE
         high = wide.astype(BF16)
         low = (wide - high.astype(F32)).astype(BF16)
         for head in range(2):
@@ -197,7 +208,7 @@
             cols = slice(head * HEAD_DIM, (head + 1) * HEAD_DIM)
             far_key[head, rows, :HEAD_DIM] = keys[:, cols]
             far_key[head, rows, HEAD_DIM:] = keys[:, cols]
-            far_value[head, rows, :] = values[:, cols]
+            far_value[head, rows, :HEAD_DIM] = values[:, cols] * WEIGHTS[level]
 
     for level in (4, 5, 3, 2):
         pltpu.make_async_copy(received(level), received(level), recv_sem.at[level - 1]).wait()
@@ -216,15 +227,15 @@
             parts = []
             for level in range(1, LEVELS + 1):
                 section = slice((level - 1) * HEAD_DIM, level * HEAD_DIM)
-                product = dot_nt(fine[level - 1, head, rows, :], far_key[head, section, :])
-                parts.append(product * SCORE_SCALE + float(level))
-            scores = jnp.concatenate(parts, axis=1)
-            top = near_top[head, rows, :][:, :1]
-            newest = jnp.maximum(top, jnp.max(scores, axis=1, keepdims=True))
+                parts.append(dot_nt(fine[level - 1, head, rows, :], far_key[head, section, :]))
+            highest = functools.reduce(jnp.maximum, parts)
+            top = near_top[head, rows, :]
+            newest = jnp.maximum(top, jnp.max(highest, axis=1, keepdims=True) + float(LEVELS))
             old = jnp.exp2(top - newest)
-            weights = jnp.exp2(scores - newest)
-            total = near_total[head, rows, :][:, :1] * old + jnp.sum(weights, axis=1, keepdims=True)
-            summed = near_sum[head, rows, :] * old + dot(weights.astype(BF16), far_value[head])
+            weights = jnp.concatenate([jnp.exp2(part - newest).astype(BF16) for part in parts], axis=1)
+            far = dot(weights, far_value[head])
+            summed = near_sum[head, rows, :] * old + far[:, :HEAD_DIM]
+            total = near_total[head, rows, :] * old + far[:, HEAD_DIM:]
             mixed.append((summed / total).astype(BF16))
         return jnp.concatenate(mixed, axis=1)
 
@@ -327,7 +338,7 @@
             pltpu.VMEM((2, ROWS, HEAD_DIM), F32),
             pltpu.VMEM((2, ROWS, HEAD_DIM), F32),
             pltpu.VMEM((2, FAR, 2 * HEAD_DIM), BF16),
-            pltpu.VMEM((2, FAR, HEAD_DIM), BF16),
+            pltpu.VMEM((2, FAR, 2 * HEAD_DIM), BF16),
             pltpu.VMEM((ROWS, MODEL), F32),
             pltpu.VMEM((14 * PARTS, PIECE, COLS), BF16),
             pltpu.VMEM((14 * PARTS, PIECE, COLS), BF16),

time: 31.6 us -> 31.6 us (level)
  no operation moved by 1% of the time
where the time goes in v5:
time: 31.6 us; the launch traced here: 31.5 us
  Pallas kernels  30.9 us (98%)
  local copies, waits for them, and re-layouts  0.66 us (2%)
    pallas_call x1, Pallas kernels, shards(): pl.pallas_call(kernel, out_shape=jax.ShapeDtypeStruct((PIECE, MODEL), BF1...  30.9 us
    unnamed x1, local copies, waits for them, and re-layouts  0.66 us

profile of v5, /device:TPU:2, one launch (start us, length us, event | category | flops | bytes accessed | tf_op | source)
XLA Modules:
  0.0 31.5 jit_solution(15818380572446292399)
XLA Ops:
  0.0 30.9 %shard_map.55 = bf16[32,2048]{1,0:T(8,128)(2,1)S(1)} custom-call(bf16[256,2048]{1,0:T(8,128)(2,1)} %tok_hbm.1, bf16[2048,256]{1,0:T(8,128)(2,1)} %wq_hbm.1, bf16[2048,256]{1,0:T(8,128)(2,1)} %wk_hbm.1, bf16[2048,256]{1,0:T(8,128)(2,1)} %wv_hbm.1, bf16[256,2048]{1,0:T(8,128)(2,1)} %wo_hbm.1), custom_call_target="tpu_custom_call" | custom-call | tf_op jit(solution)/shard_map/pallas_call | solution.py:323
  30.9 0.7 %copy.7 = bf16[32,2048]{1,0:T(8,128)(2,1)} copy(bf16[32,2048]{1,0:T(8,128)(2,1)S(1)} %shard_map.55) | data formatting | bytes 262144

commit v6 on v4

--- a/solution.py
+++ b/solution.py
@@ -77,6 +77,10 @@
 
     barrier = pltpu.get_barrier_semaphore()
 
+    up, down = (z + 1) % RING, (z + RING - 1) % RING
+    for neighbour in (up, down):
+        pl.semaphore_signal(barrier, inc=1, device_id={"head": neighbour}, device_id_type=MESH)
+
     def greet(step, carry):
         pl.semaphore_signal(
             barrier, inc=1, device_id={"seq": (me + 2 * step) % SEQ}, device_id_type=MESH
@@ -85,10 +89,6 @@
 
     lax.fori_loop(1, SEQ // 2, greet, 0)
     pl.semaphore_signal(barrier, inc=1, device_id={"seq": me ^ 1}, device_id_type=MESH)
-    up, down = (z + 1) % RING, (z + RING - 1) % RING
-    for neighbour in (up, down):
-        pl.semaphore_signal(barrier, inc=1, device_id={"head": neighbour}, device_id_type=MESH)
-
     loads = []
     for c in range(CHUNKS):
         span = pl.ds(c * DEPTH, DEPTH)
@@ -298,7 +298,7 @@
         partial[mine, columns_of(half, 0)] += ring[index].astype(F32)
     for copy in hops[-4:-2]:
         copy.wait_send()
-    for half in range(2):
+    for half in (1, 0):
         long, index = hop(half, 0, 0, 3)
         long.wait_recv()
         columns = columns_of(half, 0)

time: 31.6 us -> 31.7 us (level)
  no operation moved by 1% of the time
where the time goes in v6:
time: 31.7 us; the launch traced here: 31.4 us
  Pallas kernels  30.8 us (97%)
  local copies, waits for them, and re-layouts  0.66 us (2%)
    pallas_call x1, Pallas kernels, shards(): pl.pallas_call(kernel, out_shape=jax.ShapeDtypeStruct((PIECE, MODEL), BF1...  30.8 us
    unnamed x1, local copies, waits for them, and re-layouts  0.66 us

profile of v6, /device:TPU:2, one launch (start us, length us, event | category | flops | bytes accessed | tf_op | source)
XLA Modules:
  0.0 31.4 jit_solution(4464302255866852019)
XLA Ops:
  0.0 30.8 %shard_map.55 = bf16[32,2048]{1,0:T(8,128)(2,1)S(1)} custom-call(bf16[256,2048]{1,0:T(8,128)(2,1)} %tok_hbm.1, bf16[2048,256]{1,0:T(8,128)(2,1)} %wq_hbm.1, bf16[2048,256]{1,0:T(8,128)(2,1)} %wk_hbm.1, bf16[2048,256]{1,0:T(8,128)(2,1)} %wv_hbm.1, bf16[256,2048]{1,0:T(8,128)(2,1)} %wo_hbm.1), custom_call_target="tpu_custom_call" | custom-call | tf_op jit(solution)/shard_map/pallas_call | solution.py:312
  30.8 0.7 %copy.7 = bf16[32,2048]{1,0:T(8,128)(2,1)} copy(bf16[32,2048]{1,0:T(8,128)(2,1)S(1)} %shard_map.55) | data formatting | bytes 262144

commit v7 on v4

--- a/solution.py
+++ b/solution.py
@@ -274,7 +274,7 @@
 
     partial[...] = dot(attend(slice(0, ROWS)), wo[...])
     for part in range(PARTS):
-        for way in range(2):
+        for way in (1, 0):
             send(way, 1, part, 0)
     for number in range(1, 4):
         for chain in range(2):

time: 31.6 us -> 31.6 us (level)
  no operation moved by 1% of the time
where the time goes in v7:
time: 31.6 us; the launch traced here: 31.4 us
  Pallas kernels  30.7 us (97%)
  local copies, waits for them, and re-layouts  0.66 us (2%)
    pallas_call x1, Pallas kernels, shards(): pl.pallas_call(kernel, out_shape=jax.ShapeDtypeStruct((PIECE, MODEL), BF1...  30.7 us
    unnamed x1, local copies, waits for them, and re-layouts  0.66 us

profile of v7, /device:TPU:2, one launch (start us, length us, event | category | flops | bytes accessed | tf_op | source)
XLA Modules:
  0.0 31.4 jit_solution(11870925087934106996)
XLA Ops:
  0.0 30.7 %shard_map.55 = bf16[32,2048]{1,0:T(8,128)(2,1)S(1)} custom-call(bf16[256,2048]{1,0:T(8,128)(2,1)} %tok_hbm.1, bf16[2048,256]{1,0:T(8,128)(2,1)} %wq_hbm.1, bf16[2048,256]{1,0:T(8,128)(2,1)} %wk_hbm.1, bf16[2048,256]{1,0:T(8,128)(2,1)} %wv_hbm.1, bf16[256,2048]{1,0:T(8,128)(2,1)} %wo_hbm.1), custom_call_target="tpu_custom_call" | custom-call | tf_op jit(solution)/shard_map/pallas_call | solution.py:312
  30.7 0.7 %copy.7 = bf16[32,2048]{1,0:T(8,128)(2,1)} copy(bf16[32,2048]{1,0:T(8,128)(2,1)S(1)} %shard_map.55) | data formatting | bytes 262144
